TPU v7x, 128 devices: a whole 4x4x4 slice. The times are simulated.
128 devices in a mesh: blk: 8 (over y_lo, x), vslab: 16 (over z, y_hi, core).
Axes of the slice: x: 4, y: 4 (y_hi: 2, y_lo: 2; y = y_hi * 2 + y_lo), z: 4, core: 2. Of those that a mesh axis runs over, the one named last changes fastest.
Arguments:
- amplitudes: float32 [1024, 128, 800], P('blk', 'vslab'), may hold values from -6 to 6
- integrals: float32 [128, 800, 4096], P('vslab', None, 'blk'), may hold values from -0.01953125 to 0.01953125
- ab_energy: float32 [4096], P('blk'), may hold values from 1 to 4
- ij_energy: float32 [1024], replicated, may hold values from -4 to -1
- block_size: int32 [32], replicated, may hold values from 1 to 95, as said below
- block_owner: int32 [32], replicated, may hold values from 0 to 15, as said below
Outputs:
- amplitude_new: float32 [1024, 12288], P(None, ('blk', 'vslab'))
Inputs may be any that keep to these rules, and one draw needn't show every extreme that they name: `block_size`: the blocks of one group fill its 512 pairs exactly; every owner holds at most 96 pairs, and one owner exactly 96. `block_owner`: every owner has two blocks.
All inputs are finite; a program needn't handle non-finite values.
Results may differ from a plain program's by a relative error of at most 0.00007.
Values sent between devices are 32-bit elements; how exact they have to be, the bound alone decides.
No kernel may reach another device: no remote copies, remote signals or barrier semaphores. Data moves between devices by JAX's collectives and lax.ppermute only.
A program may use at most 128 MiB of HBM per device.

v0:
```python
import jax
import jax.numpy as jnp
from jax import lax
from jax.sharding import PartitionSpec as P


def slot_tables(block_size, block_owner, rows, owners, cap):
    count = block_size.shape[0]
    order = jnp.arange(count, dtype=jnp.int32)
    starts = jnp.cumsum(block_size) - block_size
    same = block_owner[:, None] == block_owner[None, :]
    earlier = order[None, :] < order[:, None]
    before = jnp.sum(jnp.where(same & earlier, block_size[None, :], 0), axis=1)
    owner_hot = block_owner[:, None] == jnp.arange(owners, dtype=jnp.int32)[None, :]
    load = jnp.sum(jnp.where(owner_hot, block_size[:, None], 0), axis=0)
    owner_start = jnp.cumsum(load) - load
    block_base = jnp.sum(jnp.where(owner_hot, owner_start[None, :], 0), axis=1)
    shift_by = block_base + before - starts
    row_ids = jnp.arange(rows, dtype=jnp.int32)
    inside = (row_ids[:, None] >= starts[None, :]) & (
        row_ids[:, None] < (starts + block_size)[None, :]
    )
    position = jnp.sum(jnp.where(inside, shift_by[None, :], 0), axis=1) + row_ids
    perm = jnp.zeros((rows,), jnp.int32).at[position].set(row_ids)
    slot_ids = jnp.arange(cap, dtype=jnp.int32)
    valid = slot_ids[None, :] < load[:, None]
    index = jnp.minimum(owner_start[:, None] + slot_ids[None, :], rows - 1)
    source = perm[index]
    return (perm, owner_start, load, source, valid)


def on_device(amplitudes, integrals, ab_energy, ij_energy, block_size, block_owner):
    owners = lax.axis_size("vslab")
    rows = integrals.shape[2]
    cap = 3 * rows // owners
    v_matrix = integrals.reshape(-1, rows)
    t_tile = amplitudes.reshape(amplitudes.shape[0], -1)
    ladder = jnp.dot(
        lax.all_gather(t_tile, "blk", axis=0, tiled=True),
        v_matrix,
        precision=lax.Precision.HIGHEST,
        preferred_element_type=jnp.float32,
    )
    perm, owner_start, load, source, valid = slot_tables(block_size, block_owner, rows, owners, cap)
    mine = lax.axis_index("vslab")
    my_source = lax.dynamic_index_in_dim(source, mine, 0, keepdims=False)
    my_valid = lax.dynamic_index_in_dim(valid, mine, 0, keepdims=False)
    packed = jnp.take(ladder, source.reshape(-1), axis=1)
    packed = jnp.where(valid.reshape(1, -1), packed, 0.0).reshape(ladder.shape[0], owners, cap)
    received = lax.all_to_all(packed, "vslab", split_axis=1, concat_axis=1, tiled=True)
    summed = jnp.sum(received, axis=1)
    denom = jnp.take(ab_energy, my_source)[None, :] - ij_energy[:, None]
    return jnp.where(my_valid[None, :], summed / denom, 0.0)


def solution(mesh):
    placed = (P("blk", "vslab", None), P("vslab", None, "blk"), P("blk"), P(), P(), P())
    return jax.shard_map(
        on_device, mesh=mesh, in_specs=placed, out_specs=P(None, ("blk", "vslab")), check_vma=False
    )
```

profile of v0, /device:TPU:1, one launch (start us, length us, event | category | flops | bytes accessed | tf_op | source)
XLA Modules:
  0.0 425.9 jit_solution(8877421864067574619)
XLA Ops:
  6.5 0.7 all-gather.2.cloned.1.call-update
  7.3 0.8 select_reduce_fusion.3
  8.0 0.1 copy.14
  8.2 0.1 reduce.1
  8.3 0.7 copy.13
  9.1 0.1 reduce
  9.2 0.1 compare_select_fusion.2
  9.3 0.1 reshape.231
  9.4 0.7 select_reduce_fusion.2
  10.1 0.9 select_reduce_fusion.1
  11.0 0.7 add_subtract_fusion
  11.7 0.1 select_reduce_fusion
  11.8 2.4 scatter_custom_fusion
  14.3 9.5 %gather_fusion = s32[1536]{0:T(1024)S(1)} fusion(s32[512]{0:T(512)S(1)} %scatter_custom_fusion, s32[2048]{0:T(1024)S(1)} %pad_clamp_fusion.1), kind=kCustom, calls=%fused_computation | custom fusion | bytes 18432 | tf_op jit(solution)/shard_map/gather | solution.py:28
  23.8 0.1 iota_compare_fusion.4
  23.9 250.5 %all-gather.2.cloned.1.call-done = f32[1024,6400]{0,1:T(8,128)} async-done(((f32[128,6400]{0,1:T(8,128)}), f32[1024,6400]{0,1:T(8,128)}) %all-gather.2.cloned.1.call-update) | async-done | bytes 26214416 | tf_op jit(solution)/shard_map/all_gather | solution.py:39
  274.4 45.6 %fusion.7 = f32[1024,512]{0,1:T(8,128)S(1)} fusion(f32[1024,6400]{0,1:T(8,128)} %all-gather.2.cloned.1.call-done, f32[6400,512]{1,0:T(8,128)} %bitcast.31), kind=kOutput, calls=%fused_computation.36 | convolution fusion | flops 40265318400 | bytes 41418752 | tf_op jit(solution)/shard_map/dot_general | solution.py:38
  320.0 5.8 %gather_fusion.1 = f32[1536,1024]{1,0:T(8,128)} fusion(f32[1024,512]{0,1:T(8,128)S(1)} %fusion.7, s32[2048]{0:T(1024)S(1)} %pad_clamp_fusion), kind=kCustom, calls=%fused_computation.1 | custom fusion | bytes 12589056 | tf_op jit(solution)/shard_map/jit(_take)/gather | solution.py:48
  325.8 4.9 %select_select_fusion = f32[1024,16,96]{0,2,1:T(8,128)} fusion(f32[1024,16,96]{0,2,1:T(8,128)} %bitcast.25, pred[16,96]{1,0:T(8,128)(4,1)S(1)} %get-tuple-element.8, pred[16,96]{1,0:T(8,128)(4,1)S(1)} %get-tuple-element.7), kind=kLoop, calls=%fused_computation.4 | loop fusion | flops 3145728 | bytes 12585984 | tf_op jit(solution)/shard_map/jit(_where)/select_n | solution.py:49
  330.8 10.5 %all-to-all-start = ((f32[1024,16,96]{0,2,1:T(8,128)}), f32[1024,16,96]{0,2,1:T(8,128)}, u32[]{:S(2)}, u32[]{:S(2)}) async-start(f32[1024,16,96]{0,2,1:T(8,128)} %select_select_fusion), calls=%async_computation | async-start | bytes 12582912 | tf_op jit(solution)/shard_map/all_to_all | solution.py:50
  341.3 1.3 gather_fusion.2
  342.6 72.2 %all-to-all-done = f32[1024,16,96]{0,2,1:T(8,128)} async-done(((f32[1024,16,96]{0,2,1:T(8,128)}), f32[1024,16,96]{0,2,1:T(8,128)}, u32[]{:S(2)}, u32[]{:S(2)}) %all-to-all-start) | async-done | bytes 6291488 | tf_op jit(solution)/shard_map/all_to_all | solution.py:50
  414.8 3.4 reduce_sum.52
  418.2 0.9 divide_select_fusion
  (18 shorter events, 0.3 us)
Async XLA Ops:
  6.5 334.7 %copy-start = (f32[512]{0:T(512)S(1)}, f32[512]{0:T(512)}, u32[]{:S(2)}) copy-start(f32[512]{0:T(512)} %param.8) | copy-start | bytes 6148
  6.5 267.8 %all-gather.2.cloned.1.call-start = ((), (), s32[]{:S(2)}) async-start(), calls=%async_computation.1 | async-start | bytes 29491200 | tf_op jit(solution)/shard_map/all_gather | solution.py:39
  330.8 84.0 %all-to-all-start = ((f32[1024,16,96]{0,2,1:T(8,128)}), f32[1024,16,96]{0,2,1:T(8,128)}, u32[]{:S(2)}, u32[]{:S(2)}) async-start(f32[1024,16,96]{0,2,1:T(8,128)} %select_select_fusion), calls=%async_computation | async-start | bytes 12582912 | tf_op jit(solution)/shard_map/all_to_all | solution.py:50
  341.2 76.9 %copy-start.1 = (f32[1024]{0:T(1024)S(1)}, f32[1024]{0:T(1024)}, u32[]{:S(2)}) copy-start(f32[1024]{0:T(1024)} %param.9) | copy-start | bytes 12292
Sparse Core Ops, SparseCore 0:
  8.9 265.4 all-gather.1
where the time goes:
time: 426 us
  waiting for transfers between devices  323 us (76%)
  matrix products  45.6 us (11%)
  local copies, waits for them, and re-layouts  20 us (5%)
  between operations  13.5 us (3%)
  other arithmetic  13 us (3%)
  starting transfers between devices  10.5 us (2%)
    all_gather x1, waiting for transfers between devices, on_device(): lax.all_gather(t_tile, 'blk', axis=0, tiled=True)  250 us
    all_to_all x1, waiting for transfers between devices, on_device(): lax.all_to_all(packed, 'vslab', split_axis=1, concat_axis=1, tiled=True)  72.2 us
    dot_general x1, matrix products, on_device(): jnp.dot(lax.all_gather(t_tile, 'blk', axis=0, tiled=True), v_matrix, prec...  45.6 us
    all_to_all x1, starting transfers between devices, on_device(): lax.all_to_all(packed, 'vslab', split_axis=1, concat_axis=1, tiled=True)  10.5 us
    gather x2, local copies, waits for them, and re-layouts, slot_tables(): source = perm[index]  9.54 us
  transfers between devices with their start and end apart: 2, of which 2 were waited for; matrix products, arithmetic and copies ran while one was open for 4% of the time, Pallas kernels for 0%

commit v1 on v0

--- a/solution.py
+++ b/solution.py
@@ -30,13 +30,19 @@
 
 
 def on_device(amplitudes, integrals, ab_energy, ij_energy, block_size, block_owner):
+
+    def touch_series(shard_in):
+        return jnp.concatenate(
+            lax.all_to_all(jnp.stack([shard_in] * lax.axis_size("blk"), axis=0), "blk", 0, 0), 0
+        )
+
     owners = lax.axis_size("vslab")
     rows = integrals.shape[2]
     cap = 3 * rows // owners
     v_matrix = integrals.reshape(-1, rows)
     t_tile = amplitudes.reshape(amplitudes.shape[0], -1)
     ladder = jnp.dot(
-        lax.all_gather(t_tile, "blk", axis=0, tiled=True),
+        touch_series(t_tile),
         v_matrix,
         precision=lax.Precision.HIGHEST,
         preferred_element_type=jnp.float32,

time: 426 us -> 557 us (1.31)
  the two profiles are of different devices: /device:TPU:1 before, /device:TPU:6 now
where the time goes in v1:
time: 557 us; the launch traced here: 556 us
  waiting for transfers between devices  451 us (81%)
  matrix products  45.8 us (8%)
  local copies, waits for them, and re-layouts  33.8 us (6%)
  starting transfers between devices  15.2 us (3%)
  other arithmetic  10.2 us (2%)
    all_to_all x1, waiting for transfers between devices, touch_series(): lax.all_to_all(jnp.stack([shard_in] * lax.axis_size('blk'), axis=0), 'blk...  378 us
    all_to_all x1, waiting for transfers between devices, on_device(): lax.all_to_all(packed, 'vslab', split_axis=1, concat_axis=1, tiled=True)  73 us
    dot_general x1, matrix products, on_device(): jnp.dot(touch_series(t_tile), v_matrix, precision=lax.Precision.HIGHEST,...  45.8 us
    another operation x2, local copies, waits for them, and re-layouts, touch_series(): jnp.stack([shard_in] * lax.axis_size('blk'), axis=0)  14.3 us
  transfers between devices with their start and end apart: 2, of which 2 were waited for; matrix products, arithmetic and copies ran while one was open for 3% of the time, Pallas kernels for 0%

profile of v1, /device:TPU:6, one launch (start us, length us, event | category | flops | bytes accessed | tf_op | source)
XLA Modules:
  0.0 556.5 jit_solution(12032399735614322257)
XLA Ops:
  0.0 3.4 copy.17
  3.4 10.9 %stack.3 = f32[8,128,6400]{2,1,0:T(8,128)} broadcast(f32[128,6400]{1,0:T(8,128)S(1)} %copy.17), dimensions={1,2} | broadcast | bytes 29491200 | tf_op jit(solution)/shard_map/stack | solution.py:36
  14.3 6.9 %all-to-all-start = ((f32[8,128,6400]{2,1,0:T(8,128)}), f32[8,128,6400]{2,1,0:T(8,128)}, u32[]{:S(2)}, u32[]{:S(2)}) async-start(f32[8,128,6400]{2,1,0:T(8,128)} %stack.3), calls=%async_computation | async-start | bytes 52428800 | tf_op jit(solution)/shard_map/all_to_all | solution.py:36
  21.2 0.1 select_reduce_fusion.3
  21.3 0.1 copy.16
  21.5 0.1 reduce.1
  21.6 0.1 copy.15
  21.7 0.1 reduce
  21.9 0.1 reshape.233
  22.0 0.1 select_reduce_fusion.2
  22.1 0.2 select_reduce_fusion.1
  22.3 0.1 select_reduce_fusion
  22.4 2.6 scatter_custom_fusion
  25.0 9.5 %gather_fusion = s32[1536]{0:T(1024)S(1)} fusion(s32[512]{0:T(512)S(1)} %scatter_custom_fusion, s32[2048]{0:T(1024)S(1)} %pad_clamp_fusion.1), kind=kCustom, calls=%fused_computation | custom fusion | bytes 18432 | tf_op jit(solution)/shard_map/gather | solution.py:28
  34.6 0.1 iota_compare_fusion.4
  34.7 378.2 %all-to-all-done = f32[8,128,6400]{2,1,0:T(8,128)} async-done(((f32[8,128,6400]{2,1,0:T(8,128)}), f32[8,128,6400]{2,1,0:T(8,128)}, u32[]{:S(2)}, u32[]{:S(2)}) %all-to-all-start) | async-done | bytes 26214432 | tf_op jit(solution)/shard_map/all_to_all | solution.py:36
  412.9 45.8 %fusion.7 = f32[1024,512]{0,1:T(8,128)S(1)} fusion(f32[1024,6400]{1,0:T(8,128)} %bitcast.6, f32[6400,512]{1,0:T(8,128)} %bitcast.32), kind=kOutput, calls=%fused_computation.36 | convolution fusion | flops 40265318400 | bytes 41418752 | tf_op jit(solution)/shard_map/dot_general | solution.py:44
  458.8 5.8 %gather_fusion.1 = f32[1536,1024]{1,0:T(8,128)} fusion(f32[1024,512]{0,1:T(8,128)S(1)} %fusion.7, s32[2048]{0:T(1024)S(1)} %pad_clamp_fusion), kind=kCustom, calls=%fused_computation.1 | custom fusion | bytes 12589056 | tf_op jit(solution)/shard_map/jit(_take)/gather | solution.py:54
  464.6 4.9 select_select_fusion
  469.6 8.3 %all-to-all-start.1 = ((f32[1024,16,96]{0,2,1:T(8,128)}), f32[1024,16,96]{0,2,1:T(8,128)}, u32[]{:S(2)}, u32[]{:S(2)}) async-start(f32[1024,16,96]{0,2,1:T(8,128)} %select_select_fusion), calls=%async_computation.1 | async-start | bytes 12582912 | tf_op jit(solution)/shard_map/all_to_all | solution.py:56
  477.9 1.3 gather_fusion.2
  479.3 73.0 %all-to-all-done.1 = f32[1024,16,96]{0,2,1:T(8,128)} async-done(((f32[1024,16,96]{0,2,1:T(8,128)}), f32[1024,16,96]{0,2,1:T(8,128)}, u32[]{:S(2)}, u32[]{:S(2)}) %all-to-all-start.1) | async-done | bytes 6291488 | tf_op jit(solution)/shard_map/all_to_all | solution.py:56
  552.2 3.4 reduce_sum.52
  555.6 0.9 divide_select_fusion
  (23 shorter events, 0.4 us)
Async XLA Ops:
  0.0 477.9 %copy-start = (f32[512]{0:T(512)S(1)}, f32[512]{0:T(512)}, u32[]{:S(2)}) copy-start(f32[512]{0:T(512)} %param.8) | copy-start | bytes 6148
  14.3 6.9 %copy-start.1 = (s32[32]{0:T(128)S(1)}, s32[32]{0:T(128)}, u32[]{:S(2)}) copy-start(s32[32]{0:T(128)} %param.10) | copy-start | bytes 388
  14.3 6.9 %copy-start.3 = (s32[32]{0:T(128)S(1)}, s32[32]{0:T(128)}, u32[]{:S(2)}) copy-start(s32[32]{0:T(128)} %param.11) | copy-start | bytes 388
  14.3 398.6 %all-to-all-start = ((f32[8,128,6400]{2,1,0:T(8,128)}), f32[8,128,6400]{2,1,0:T(8,128)}, u32[]{:S(2)}, u32[]{:S(2)}) async-start(f32[8,128,6400]{2,1,0:T(8,128)} %stack.3), calls=%async_computation | async-start | bytes 52428800 | tf_op jit(solution)/shard_map/all_to_all | solution.py:36
  469.6 82.7 %all-to-all-start.1 = ((f32[1024,16,96]{0,2,1:T(8,128)}), f32[1024,16,96]{0,2,1:T(8,128)}, u32[]{:S(2)}, u32[]{:S(2)}) async-start(f32[1024,16,96]{0,2,1:T(8,128)} %select_select_fusion), calls=%async_computation.1 | async-start | bytes 12582912 | tf_op jit(solution)/shard_map/all_to_all | solution.py:56
  477.9 77.7 %copy-start.2 = (f32[1024]{0:T(1024)S(1)}, f32[1024]{0:T(1024)}, u32[]{:S(2)}) copy-start(f32[1024]{0:T(1024)} %param.9) | copy-start | bytes 12292
